TPU v7x, 256 devices: a whole 4x4x8 slice. The times are simulated.
256 devices in a mesh: expert: 64 (over z, y, core), tensor: 4 (over x).
Axes of the slice: x: 4, y: 4, z: 8, core: 2. Of those that a mesh axis runs over, the one named last changes fastest.
Arguments:
- attn_heads: bfloat16 [32768, 2048], P('expert', 'tensor'), may hold values from -6 to 6
- o_weight: bfloat16 [2048, 2048], P('tensor'), may hold values from -0.125 to 0.125
- resid: bfloat16 [32768, 2048], P(('expert', 'tensor')), may hold values from -6 to 6
- norm_gain: float32 [2048], replicated, may hold values from 0.1 to 1.9
- expert_ids: int32 [32768, 4], P(('expert', 'tensor')), may hold values from 0 to 63, all different within a row; in each aligned block of 128 rows (0 to 127, 128 to 255, ...) at most 11 rows name the same one
- combine_weights: float32 [32768, 4], P(('expert', 'tensor')), may hold values from 0.05 to 0.35
- w_gate_up: bfloat16 [64, 2, 2048, 1408], P('expert', None, None, 'tensor'), may hold values from -0.125 to 0.125
- w_down: bfloat16 [64, 1408, 2048], P('expert', 'tensor'), may hold values from -0.15625 to 0.15625
Outputs:
- layer_out: bfloat16 [32768, 2048], P(('expert', 'tensor'))
Inputs may be any that keep to these rules, and one draw needn't show every extreme that they name: `expert_ids`: each row names 4 different experts. In the rows of one device (128 aligned rows) no expert is named more than 11 times, and in some device's rows one expert is named exactly 11 times.
All inputs are finite; a program needn't handle non-finite values.
Results may differ from a plain program's by a relative error of at most 0.015.
Values may be sent and summed in bfloat16 or wider, within the bound.
A program may use at most 128 MiB of HBM per device.

v0:
```python
import jax
import jax.numpy as jnp
from jax import lax
from jax.sharding import PartitionSpec as P

eps_norm = 1e-06


def swiglu(inputs, gate_cols, up_cols):
    gate_val = jnp.dot(inputs, gate_cols, preferred_element_type=jnp.float32)
    up_value = jnp.dot(inputs, up_cols, preferred_element_type=jnp.float32)
    return (jax.nn.silu(gate_val) * up_value).astype(jnp.bfloat16)


def send_back(results):
    return lax.all_to_all(results, "expert", split_axis=0, concat_axis=0, tiled=True)


def on_device(
    attn_heads, o_weight, resid, norm_gain, expert_ids, combine_weights, w_gate_up, w_down
):
    tok_rows = resid.shape[0]
    width = resid.shape[1]
    top_count = expert_ids.shape[1]
    num_experts = w_gate_up.shape[0] * lax.axis_size("expert")
    capacity = max(
        2, min(tok_rows, (4 * tok_rows * top_count + 3 * num_experts - 1) // (3 * num_experts))
    )
    attn_out = lax.psum_scatter(
        jnp.dot(attn_heads, o_weight, preferred_element_type=jnp.float32).astype(jnp.bfloat16),
        "tensor",
        scatter_dimension=0,
        tiled=True,
    ).astype(jnp.float32)
    mixed = resid.astype(jnp.float32) + attn_out
    scale = lax.rsqrt(jnp.mean(mixed * mixed, axis=1, keepdims=True) + eps_norm)
    normed = (mixed * scale * norm_gain[None, :]).astype(jnp.bfloat16)
    pair_expert = expert_ids.reshape(-1)
    onehot = (pair_expert[:, None] == jnp.arange(num_experts, dtype=jnp.int32)[None, :]).astype(
        jnp.int32
    )
    slot_rank = jnp.sum((jnp.cumsum(onehot, axis=0) - onehot) * onehot, axis=1)
    slot_index = pair_expert * capacity + slot_rank
    pair_token = jnp.arange(tok_rows * top_count, dtype=jnp.int32) // top_count
    outgoing = (
        jnp.zeros((num_experts * capacity, width), jnp.bfloat16)
        .at[slot_index]
        .set(normed[pair_token])
    )
    outgoing = outgoing.reshape(num_experts, capacity, width)
    received = lax.all_to_all(outgoing, "expert", split_axis=0, concat_axis=0, tiled=True)
    slot_rows = received.reshape(-1, width)
    gathered = lax.all_gather(slot_rows, "tensor", axis=0, tiled=True)
    hidden = swiglu(gathered, w_gate_up[0, 0], w_gate_up[0, 1])
    total = lax.psum_scatter(
        jnp.dot(hidden, w_down[0], preferred_element_type=jnp.float32).astype(jnp.bfloat16),
        "tensor",
        scatter_dimension=0,
        tiled=True,
    )
    returned = send_back(total.reshape(received.shape))
    picked = returned.reshape(num_experts * capacity, width)[slot_index].reshape(
        tok_rows, top_count, width
    )
    moe_out = jnp.zeros((tok_rows, width), jnp.float32)
    for top_slot in range(top_count):
        moe_out = moe_out + combine_weights[:, top_slot : top_slot + 1] * picked[
            :, top_slot
        ].astype(jnp.float32)
    return (mixed + moe_out).astype(jnp.bfloat16)


def solution(mesh):
    in_specs = (
        P("expert", "tensor"),
        P("tensor", None),
        P(("expert", "tensor"), None),
        P(),
        P(("expert", "tensor"), None),
        P(("expert", "tensor"), None),
        P("expert", None, None, "tensor"),
        P("expert", "tensor", None),
    )
    out_specs = P(("expert", "tensor"), None)
    return jax.shard_map(
        on_device, mesh=mesh, in_specs=in_specs, out_specs=out_specs, check_vma=False
    )
```

profile of v0, /device:TPU:2, one launch (start us, length us, event | category | flops | bytes accessed | tf_op | source)
XLA Modules:
  0.0 551.9 jit_solution(2199957552460650922)
XLA Ops:
  6.5 1.6 copy-done
  8.1 3.7 convolution_convert_fusion.1
  12.2 1.2 reduce-window.6
  13.4 0.2 slice_reduce_fusion
  13.7 0.1 copy.9
  14.1 31.8 %reduce-scatter.3.cloned.1.call-done = bf16[128,2048]{1,0:T(8,128)(2,1)} async-done(((bf16[512,2048]{1,0:T(8,128)(2,1)}), bf16[128,2048]{1,0:T(8,128)(2,1)}) %reduce-scatter.3.cloned.1.call-update) | async-done | bytes 524304 | tf_op jit(solution)/shard_map/reduce_scatter | solution.py:29
  45.9 1.3 multiply_reduce_fusion
  47.2 2.0 multiply_convert_fusion
  49.2 10.6 %scatter_custom_fusion = bf16[704,2048]{1,0:T(8,128)(2,1)S(1)} fusion(s32[512]{0:T(512)S(1)} %bitcast.65, bf16[128,2048]{1,0:T(8,128)(2,1)} %multiply_convert_fusion, s32[1024]{0:T(1024)S(1)} %pad_clamp_fusion.1, bf16[]{:T(256)} %constant.29.clone.1), kind=kCustom, calls=%fused_computation.7 | custom fusion | bytes 2884096 | tf_op jit(solution)/shard_map/scatter | solution.py:48
  59.9 2.9 reshape.122
  62.7 107.1 %all_to_all.10 = bf16[64,11,2048]{2,1,0:T(8,128)(2,1)} all-to-all(bf16[64,11,2048]{2,1,0:T(8,128)(2,1)} %reshape.122), channel_id=1, replica_groups=mesh['expert'=64,'tensor'=4] {'expert'}, dimensions={0} | all-to-all | bytes 5767168 | tf_op jit(solution)/shard_map/all_to_all | solution.py:51
  169.8 4.8 reshape.123
  174.7 108.3 %all-gather.2.cloned.1.call-done = bf16[2816,2048]{1,0:T(8,128)(2,1)} async-done(((bf16[704,2048]{1,0:T(8,128)(2,1)}), bf16[2816,2048]{1,0:T(8,128)(2,1)}) %all-gather.2.cloned.1.call-update) | async-done | bytes 11534352 | tf_op jit(solution)/shard_map/all_gather | solution.py:53
  282.9 9.1 %fusion.7 = f32[2816,352]{0,1:T(8,128)} fusion(bf16[2816,2048]{1,0:T(8,128)(2,1)} %all-gather.2.cloned.1.call-done, bf16[1,2,2048,352]{2,3,1,0:T(8,128)(2,1)S(1)} %copy-done.7), kind=kOutput, calls=%fused_computation.12 | convolution fusion | flops 4060086272 | bytes 16941056 | tf_op jit(solution)/shard_map/dot_general | solution.py:10
  292.1 17.3 %convolution_convert_fusion = bf16[2816,2048]{1,0:T(8,128)(2,1)} fusion(bf16[2816,2048]{1,0:T(8,128)(2,1)} %all-gather.2.cloned.1.call-done, f32[2816,352]{0,1:T(8,128)} %fusion.7, bf16[1,352,2048]{2,1,0:T(8,128)(2,1)} %param.15, bf16[1,2,2048,352]{2,3,1,0:T(8,128)(2,1)S(1)} %copy-done.7), kind=kOutput, calls=%fused_computation.3 | convolution fusion | flops 8131887104 | bytes 29917184 | tf_op jit(solution)/shard_map/dot_general | solution.py:56
  309.4 108.4 %reduce-scatter.5.cloned.1.call-done = bf16[704,2048]{1,0:T(8,128)(2,1)} async-done(((bf16[2816,2048]{1,0:T(8,128)(2,1)}), bf16[704,2048]{1,0:T(8,128)(2,1)}) %reduce-scatter.5.cloned.1.call-update) | async-done | bytes 2883600 | tf_op jit(solution)/shard_map/reduce_scatter | solution.py:55
  417.8 4.8 reshape.124
  422.6 11.1 %all-to-all-start.1 = ((bf16[64,11,2048]{2,1,0:T(8,128)(2,1)}), bf16[64,11,2048]{2,1,0:T(8,128)(2,1)}, u32[]{:S(2)}, u32[]{:S(2)}) async-start(bf16[64,11,2048]{2,1,0:T(8,128)(2,1)} %reshape.124), calls=%async_computation.3 | async-start | bytes 8388608 | tf_op jit(solution)/shard_map/all_to_all | solution.py:16
  433.7 96.0 %all-to-all-done.1 = bf16[64,11,2048]{2,1,0:T(8,128)(2,1)} async-done(((bf16[64,11,2048]{2,1,0:T(8,128)(2,1)}), bf16[64,11,2048]{2,1,0:T(8,128)(2,1)}, u32[]{:S(2)}, u32[]{:S(2)}) %all-to-all-start.1) | async-done | bytes 2883616 | tf_op jit(solution)/shard_map/all_to_all | solution.py:16
  529.7 3.4 reshape.125
  533.1 3.3 gather_fusion
  536.4 2.7 reshape.126
  539.2 3.1 fusion.23
  542.3 3.1 fusion.15
  (36 shorter events, 0.8 us)
Async XLA Ops:
  6.5 1.6 copy-start
  6.5 5.3 copy-start.5
  6.5 39.3 %reduce-scatter.3.cloned.1.call-start = ((), (), s32[]{:S(2)}) async-start(), calls=%async_computation.4 | async-start | bytes 2621440 | tf_op jit(solution)/shard_map/reduce_scatter | solution.py:29
  11.8 34.1 %copy-start.2 = (bf16[128,2048]{1,0:T(8,128)(2,1)S(1)}, bf16[128,2048]{1,0:T(8,128)(2,1)}, u32[]{:S(2)}) copy-start(bf16[128,2048]{1,0:T(8,128)(2,1)} %param.10) | copy-start | bytes 1572868
  11.8 35.4 %copy-start.4 = (f32[2048]{0:T(1024)S(1)}, f32[2048]{0:T(1024)}, u32[]{:S(2)}) copy-start(f32[2048]{0:T(1024)} %param.11) | copy-start | bytes 24580
  11.8 271.1 %all-gather.2.cloned.1.call-start = ((), (), s32[]{:S(2)}) async-start(), calls=%async_computation.5 | async-start | bytes 14417920 | tf_op jit(solution)/shard_map/all_gather | solution.py:53
  174.6 108.3 %copy-start.7 = (bf16[1,2,2048,352]{2,3,1,0:T(8,128)(2,1)S(1)}, bf16[1,2,2048,352]{2,3,1,0:T(8,128)(2,1)}, u32[]{:S(2)}) copy-start(bf16[1,2,2048,352]{2,3,1,0:T(8,128)(2,1)} %param.14) | copy-start | bytes 8650756
  174.6 243.2 %reduce-scatter.5.cloned.1.call-start = ((), (), s32[]{:S(2)}) async-start(), calls=%async_computation.6 | async-start | bytes 14417920 | tf_op jit(solution)/shard_map/reduce_scatter | solution.py:55
  422.6 11.1 %copy-start.6 = (f32[128,4]{0,1:T(4,128)S(1)}, f32[128,4]{0,1:T(4,128)}, u32[]{:S(2)}) copy-start(f32[128,4]{0,1:T(4,128)} %param.13) | copy-start | bytes 6148
  422.6 107.1 %all-to-all-start.1 = ((bf16[64,11,2048]{2,1,0:T(8,128)(2,1)}), bf16[64,11,2048]{2,1,0:T(8,128)(2,1)}, u32[]{:S(2)}, u32[]{:S(2)}) async-start(bf16[64,11,2048]{2,1,0:T(8,128)(2,1)} %reshape.124), calls=%async_computation.3 | async-start | bytes 8388608 | tf_op jit(solution)/shard_map/all_to_all | solution.py:16
  539.2 3.1 copy-start.3
  542.3 3.1 copy-start.1
Sparse Core Ops, SparseCore 0:
  11.9 33.9 reduce-scatter.2
  174.8 108.1 all-gather.1
  309.5 108.2 reduce-scatter.4
where the time goes:
time: 554 us; the launch traced here: 552 us
  waiting for transfers between devices  344 us (62%)
  blocking collectives  107 us (19%)
  local copies, waits for them, and re-layouts  38 us (7%)
  matrix products  30.1 us (5%)
  between operations  13.3 us (2%)
  starting transfers between devices  11.2 us (2%)
  other arithmetic  7.85 us (1%)
    reduce_scatter x1, waiting for transfers between devices, on_device(): lax.psum_scatter(jnp.dot(hidden, w_down[0], preferred_element_type=jnp.fl...  108 us
    all_gather x1, waiting for transfers between devices, on_device(): gathered = lax.all_gather(slot_rows, 'tensor', axis=0, tiled=True)  108 us
    all_to_all x1, blocking collectives, on_device(): lax.all_to_all(outgoing, 'expert', split_axis=0, concat_axis=0, tiled=True)  107 us
    all_to_all x1, waiting for transfers between devices, send_back(): lax.all_to_all(results, 'expert', split_axis=0, concat_axis=0, tiled=True)  96 us
    reduce_scatter x1, waiting for transfers between devices, on_device(): lax.psum_scatter(jnp.dot(attn_heads, o_weight, preferred_element_type=jnp...  31.8 us
    dot_general x1, matrix products, on_device(): jnp.dot(hidden, w_down[0], preferred_element_type=jnp.float32)  17.3 us
    all_to_all x1, starting transfers between devices, send_back(): lax.all_to_all(results, 'expert', split_axis=0, concat_axis=0, tiled=True)  11.1 us
  transfers between devices with their start and end apart: 4, of which 4 were waited for; matrix products, arithmetic and copies ran while one was open for 0% of the time, Pallas kernels for 0%

commit v1 on v0

v1 whole, which is shorter than its diff:
```python
import jax
import jax.numpy as jnp
from jax import lax
from jax.sharding import PartitionSpec as P

eps_norm = 1e-06


def on_device(
    attn_heads, o_weight, resid, norm_gain, expert_ids, combine_weights, w_gate_up, w_down
):
    tok_rows, width = resid.shape
    top_count = expert_ids.shape[1]
    num_experts = w_gate_up.shape[0] * lax.axis_size("expert")
    capacity = max(
        2, min(tok_rows, (4 * tok_rows * top_count + 3 * num_experts - 1) // (3 * num_experts))
    )
    partial = jnp.dot(attn_heads, o_weight, preferred_element_type=jnp.float32).astype(jnp.bfloat16)
    attn_out = lax.psum_scatter(partial, "tensor", scatter_dimension=0, tiled=True)
    gate_up_all = lax.all_gather(jnp.swapaxes(w_gate_up[0], 1, 2), "tensor", axis=0)
    down_all = lax.all_gather(w_down[0], "tensor", axis=0, tiled=True)
    mixed = resid.astype(jnp.float32) + attn_out.astype(jnp.float32)
    scale = lax.rsqrt(jnp.mean(mixed * mixed, axis=1, keepdims=True) + eps_norm)
    normed = (mixed * scale * norm_gain[None, :]).astype(jnp.bfloat16)

    named = expert_ids[:, :, None] == jnp.arange(num_experts, dtype=jnp.int32)[None, None, :]
    holds = jnp.any(named, axis=1)
    row = jnp.arange(tok_rows, dtype=jnp.int32)
    earlier = (row[None, :] < row[:, None]).astype(jnp.bfloat16)
    rank = jnp.dot(earlier, holds.astype(jnp.bfloat16), preferred_element_type=jnp.float32)
    rank = jnp.where(holds, rank.astype(jnp.int32), -1)
    weight = jnp.sum(jnp.where(named, combine_weights[:, :, None], 0.0), axis=1)
    slot = jnp.arange(capacity, dtype=jnp.int32)
    place = rank[:, :, None] == slot[None, None, :]
    pick = place.astype(jnp.bfloat16).reshape(tok_rows, num_experts * capacity)
    outgoing = lax.dot_general(
        pick, normed, (((0,), (0,)), ((), ())), preferred_element_type=jnp.float32
    ).astype(jnp.bfloat16)
    received = lax.all_to_all(
        outgoing.reshape(num_experts, capacity, width), "expert", split_axis=0, concat_axis=0, tiled=True
    ).reshape(-1, width)
    total = jnp.zeros(received.shape, jnp.float32)
    gate = lax.dot_general(
        received, gate_up_all[:, 0].reshape(-1, width), (((1,), (1,)), ((), ())),
        preferred_element_type=jnp.float32,
    )
    up = lax.dot_general(
        received, gate_up_all[:, 1].reshape(-1, width), (((1,), (1,)), ((), ())),
        preferred_element_type=jnp.float32,
    )
    hidden = (jax.nn.silu(gate) * up).astype(jnp.bfloat16)
    total = jnp.dot(hidden, down_all, preferred_element_type=jnp.float32).astype(jnp.bfloat16)
    returned = lax.all_to_all(
        total.reshape(num_experts, capacity, width), "expert", split_axis=0, concat_axis=0, tiled=True
    ).reshape(-1, width)
    spread = jnp.where(place, weight[:, :, None], 0.0).reshape(tok_rows, num_experts * capacity)
    high = spread.astype(jnp.bfloat16)
    low = (spread - high.astype(jnp.float32)).astype(jnp.bfloat16)
    moe_out = jnp.dot(high, returned, preferred_element_type=jnp.float32) + jnp.dot(
        low, returned, preferred_element_type=jnp.float32
    )
    return (mixed + moe_out).astype(jnp.bfloat16)


def solution(mesh):
    in_specs = (
        P("expert", "tensor"),
        P("tensor", None),
        P(("expert", "tensor"), None),
        P(),
        P(("expert", "tensor"), None),
        P(("expert", "tensor"), None),
        P("expert", None, None, "tensor"),
        P("expert", "tensor", None),
    )
    out_specs = P(("expert", "tensor"), None)
    return jax.shard_map(
        on_device, mesh=mesh, in_specs=in_specs, out_specs=out_specs, check_vma=False
    )
```

time: 554 us -> 376 us (0.68)
  waiting for transfers between devices: 344 us -> 168 us
  matrix products: 30.1 us -> 47.1 us
  local copies, waits for them, and re-layouts: 38 us -> 27.8 us
  other arithmetic: 7.85 us -> 1.34 us
    reduce_scatter x2 -> x1, waiting for transfers between devices: 140 us -> 32.1 us  [on_device(): lax.psum_scatter(partial, 'tensor', scatter_dimension=0, tiled=True)]
    all_gather x1 -> x2, waiting for transfers between devices: 108 us -> 38.4 us  [the longest x1 38.4 us: on_device(): down_all = lax.all_gather(w_down[0], 'tensor', axis=0, tiled=True)]
    dot_general x2 -> x6, matrix products: 26.4 us -> 43.4 us  [the longest x1 17.3 us: on_device(): jnp.dot(hidden, down_all, preferred_element_type=jnp.float32)]
    scatter x1 -> x0, local copies, waits for them, and re-layouts: 10.6 us -> none  [on_device(): outgoing = jnp.zeros((num_experts * capacity, width), jnp.bfloat16).at[sl...]
    slice x2 -> x1, local copies, waits for them, and re-layouts: 3.3 us -> 11.6 us  [on_device(): gate_up_all[:, 1].reshape(-1, width)]
    reshape x5 -> x3, local copies, waits for them, and re-layouts: 18.6 us -> 14.3 us  [the longest x1 4.81 us: on_device(): received = lax.all_to_all(outgoing.reshape(num_experts, capacity, width),...]
  transfers between devices with their start and end apart: 4 -> 4, of which waited for: 4 -> 3; matrix products, arithmetic and copies ran while one was open for 0% -> 10% of each run, Pallas kernels for 0% -> 0%
where the time goes in v1:
time: 376 us; the launch traced here: 375 us
  waiting for transfers between devices  168 us (45%)
  blocking collectives  107 us (28%)
  matrix products  47.1 us (13%)
  local copies, waits for them, and re-layouts  27.8 us (7%)
  between operations  13.2 us (4%)
  starting transfers between devices  10.9 us (3%)
    all_to_all x1, blocking collectives, on_device(): lax.all_to_all(outgoing.reshape(num_experts, capacity, width), 'expert',...  107 us
    all_to_all x1, waiting for transfers between devices, on_device(): lax.all_to_all(total.reshape(num_experts, capacity, width), 'expert', spl...  96.2 us
    all_gather x1, waiting for transfers between devices, on_device(): down_all = lax.all_gather(w_down[0], 'tensor', axis=0, tiled=True)  38.4 us
    reduce_scatter x1, waiting for transfers between devices, on_device(): lax.psum_scatter(partial, 'tensor', scatter_dimension=0, tiled=True)  32.1 us
    dot_general x1, matrix products, on_device(): jnp.dot(hidden, down_all, preferred_element_type=jnp.float32)  17.3 us
    slice x1, local copies, waits for them, and re-layouts, on_device(): gate_up_all[:, 1].reshape(-1, width)  11.6 us
    all_to_all x1, starting transfers between devices, on_device(): lax.all_to_all(total.reshape(num_experts, capacity, width), 'expert', spl...  10.9 us
    dot_general x1, matrix products, on_device(): lax.dot_general(received, gate_up_all[:, 0].reshape(-1, width), (((1,), (...  10.4 us
  transfers between devices with their start and end apart: 4, of which 3 were waited for; matrix products, arithmetic and copies ran while one was open for 10% of the time, Pallas kernels for 0%

profile of v1, /device:TPU:2, one launch (start us, length us, event | category | flops | bytes accessed | tf_op | source)
XLA Modules:
  0.0 375.3 jit_solution(17430441759420197268)
XLA Ops:
  6.5 1.6 copy-done
  8.1 3.7 convolution_convert_fusion.1
  11.8 0.0 reduce-scatter.2.cloned.1.call-update
  11.8 0.0 all-gather.5.cloned.1.call-start
  11.9 0.7 all-gather.5.cloned.1.call-update
  12.6 0.0 all-gather.7.cloned.1.call-start
  12.6 0.7 all-gather.7.cloned.1.call-update
  13.3 0.1 eq.48
  13.5 0.1 fusion.10
  13.7 32.1 %reduce-scatter.2.cloned.1.call-done = bf16[128,2048]{1,0:T(8,128)(2,1)} async-done(((bf16[512,2048]{1,0:T(8,128)(2,1)}), bf16[128,2048]{1,0:T(8,128)(2,1)}) %reduce-scatter.2.cloned.1.call-update) | async-done | bytes 524304 | tf_op jit(solution)/shard_map/reduce_scatter | solution.py:19
  45.9 1.3 multiply_reduce_fusion
  47.2 3.6 convolution_convert_fusion
  50.8 4.8 %reshape.42 = bf16[64,11,2048]{2,1,0:T(8,128)(2,1)} reshape(bf16[704,2048]{1,0:T(8,128)(2,1)} %convolution_convert_fusion) | data formatting | bytes 5767168 | tf_op jit(solution)/shard_map/reshape | solution.py:40
  55.6 106.9 %all_to_all.10 = bf16[64,11,2048]{2,1,0:T(8,128)(2,1)} all-to-all(bf16[64,11,2048]{2,1,0:T(8,128)(2,1)} %reshape.42), channel_id=1, replica_groups=mesh['expert'=64,'tensor'=4] {'expert'}, dimensions={0} | all-to-all | bytes 5767168 | tf_op jit(solution)/shard_map/all_to_all | solution.py:39
  162.5 4.8 %reshape.43 = bf16[704,2048]{1,0:T(8,128)(2,1)} reshape(bf16[64,11,2048]{2,1,0:T(8,128)(2,1)} %all_to_all.10) | data formatting | bytes 5767168 | tf_op jit(solution)/shard_map/reshape | solution.py:41
  167.3 11.6 %fusion.26 = (bf16[4,1,352,2048]{3,2,1,0:T(8,128)(2,1)}, bf16[4,1,352,2048]{3,2,1,0:T(8,128)(2,1)}) fusion(bf16[4,2,352,2048]{3,2,1,0:T(8,128)(2,1)} %bitcast.39), kind=kLoop, calls=%fused_computation.39 | loop fusion | bytes 23068672 | tf_op jit(solution)/shard_map/slice | solution.py:48
  178.9 10.4 %fusion.27 = f32[704,1408]{1,0:T(8,128)} fusion(bf16[704,2048]{1,0:T(8,128)(2,1)} %reshape.43, bf16[1408,2048]{1,0:T(8,128)(2,1)} %bitcast.41), kind=kOutput, calls=%fused_computation.40 | convolution fusion | flops 4060086272 | bytes 12615680 | tf_op jit(solution)/shard_map/dot_general | solution.py:43
  189.3 38.4 %all-gather.7.cloned.1.call-done = bf16[1,1408,2048]{2,1,0:T(8,128)(2,1)} async-done(((bf16[1,352,2048]{2,1,0:T(8,128)(2,1)}), bf16[1,1408,2048]{2,1,0:T(8,128)(2,1)}) %all-gather.7.cloned.1.call-update) | async-done | bytes 5767184 | tf_op jit(solution)/shard_map/all_gather | solution.py:21
  227.6 17.3 %fusion.2 = bf16[704,2048]{1,0:T(8,128)(2,1)} fusion(bf16[1,1408,2048]{2,1,0:T(8,128)(2,1)} %all-gather.7.cloned.1.call-done, f32[704,1408]{1,0:T(8,128)} %fusion.27, bf16[704,2048]{1,0:T(8,128)(2,1)} %reshape.43, bf16[1408,2048]{1,0:T(8,128)(2,1)} %bitcast.40), kind=kOutput, calls=%fused_computation.4 | convolution fusion | flops 8127561728 | bytes 21266432 | tf_op jit(solution)/shard_map/dot_general | solution.py:52
  245.0 4.8 %reshape.44 = bf16[64,11,2048]{2,1,0:T(8,128)(2,1)} reshape(bf16[704,2048]{1,0:T(8,128)(2,1)} %fusion.2) | data formatting | bytes 5767168 | tf_op jit(solution)/shard_map/reshape | solution.py:54
  249.7 10.9 %all-to-all-start.1 = ((bf16[64,11,2048]{2,1,0:T(8,128)(2,1)}), bf16[64,11,2048]{2,1,0:T(8,128)(2,1)}, u32[]{:S(2)}, u32[]{:S(2)}) async-start(bf16[64,11,2048]{2,1,0:T(8,128)(2,1)} %reshape.44), calls=%async_computation.2 | async-start | bytes 8388608 | tf_op jit(solution)/shard_map/all_to_all | solution.py:53
  260.6 96.2 %all-to-all-done.1 = bf16[64,11,2048]{2,1,0:T(8,128)(2,1)} async-done(((bf16[64,11,2048]{2,1,0:T(8,128)(2,1)}), bf16[64,11,2048]{2,1,0:T(8,128)(2,1)}, u32[]{:S(2)}, u32[]{:S(2)}) %all-to-all-start.1) | async-done | bytes 2883616 | tf_op jit(solution)/shard_map/all_to_all | solution.py:53
  356.8 5.5 %convolution_bitcast_fusion = f32[128,2048]{1,0:T(8,128)S(1)} fusion(bf16[64,11,2048]{2,1,0:T(8,128)(2,1)} %all-to-all-done.1, f32[128,64]{0,1:T(8,128)S(1)} %select_reduce_fusion, s32[128,64]{0,1:T(8,128)S(1)} %fusion.10), kind=kOutput, calls=%fused_computation.6 | convolution fusion | flops 369639424 | bytes 3997696 | tf_op jit(solution)/shard_map/dot_general | solution.py:59
  362.4 6.4 %fusion.7 = bf16[128,2048]{1,0:T(8,128)(2,1)} fusion(f32[128,2048]{1,0:T(8,128)S(1)} %convolution_bitcast_fusion, bf16[64,11,2048]{2,1,0:T(8,128)(2,1)} %all-to-all-done.1, bf16[128,2048]{1,0:T(8,128)(2,1)S(1)} %copy-done.3, bf16[128,2048]{1,0:T(8,128)(2,1)S(1)} %copy-done.2, f32[128,64]{0,1:T(8,128)S(1)} %select_reduce_fusion, s32[128,64]{0,1:T(8,128)S(1)} %fusion.10), kind=kOutput, calls=%fused_computation.10 | convolution fusion | flops 370851840 | bytes 5570560 | tf_op jit(solution)/shard_map/dot_general | solution.py:59
  (21 shorter events, 0.2 us)
Async XLA Ops:
  6.5 1.6 copy-start
  6.5 39.3 %reduce-scatter.2.cloned.1.call-start = ((), (), s32[]{:S(2)}) async-start(), calls=%async_computation.3 | async-start | bytes 2621440 | tf_op jit(solution)/shard_map/reduce_scatter | solution.py:19
  11.8 1.7 copy-start.5
  11.8 34.1 %copy-start.2 = (bf16[128,2048]{1,0:T(8,128)(2,1)S(1)}, bf16[128,2048]{1,0:T(8,128)(2,1)}, u32[]{:S(2)}) copy-start(bf16[128,2048]{1,0:T(8,128)(2,1)} %param.10) | copy-start | bytes 1572868
  11.8 35.4 %copy-start.4 = (f32[2048]{0:T(1024)S(1)}, f32[2048]{0:T(1024)}, u32[]{:S(2)}) copy-start(f32[2048]{0:T(1024)} %param.11) | copy-start | bytes 24580
  11.8 155.5 %all-gather.5.cloned.1.call-start = ((), (), s32[]{:S(2)}) async-start(), calls=%async_computation.4 | async-start | bytes 14417920 | tf_op jit(solution)/shard_map/all_gather | solution.py:20
  12.6 215.0 %all-gather.7.cloned.1.call-start = ((), (), s32[]{:S(2)}) async-start(), calls=%async_computation.5 | async-start | bytes 7208960 | tf_op jit(solution)/shard_map/all_gather | solution.py:21
  249.7 10.9 %copy-start.6 = (f32[128,4]{0,1:T(4,128)S(1)}, f32[128,4]{0,1:T(4,128)}, u32[]{:S(2)}) copy-start(f32[128,4]{0,1:T(4,128)} %param.13) | copy-start | bytes 6148
  249.7 107.1 %all-to-all-start.1 = ((bf16[64,11,2048]{2,1,0:T(8,128)(2,1)}), bf16[64,11,2048]{2,1,0:T(8,128)(2,1)}, u32[]{:S(2)}, u32[]{:S(2)}) async-start(bf16[64,11,2048]{2,1,0:T(8,128)(2,1)} %reshape.44), calls=%async_computation.2 | async-start | bytes 8388608 | tf_op jit(solution)/shard_map/all_to_all | solution.py:53
  260.6 101.8 %copy-start.3 = (bf16[128,2048]{1,0:T(8,128)(2,1)S(1)}, bf16[128,2048]{1,0:T(8,128)(2,1)}, u32[]{:S(2)}) copy-start(bf16[128,2048]{1,0:T(8,128)(2,1)} %reduce-scatter.2.cloned.1.call-done) | copy-start | bytes 1572868
  260.6 108.2 %copy-start.1 = (bf16[512,2048]{1,0:T(8,128)(2,1)S(1)}, bf16[512,2048]{1,0:T(8,128)(2,1)}, u32[]{:S(2)}) copy-start(bf16[512,2048]{1,0:T(8,128)(2,1)} %param.9) | copy-start | bytes 6291460
Sparse Core Ops, SparseCore 0:
  11.9 33.9 reduce-scatter.1
  47.8 113.2 all-gather.4
  163.1 64.4 all-gather.6

commit v2 on v1

v2 whole, which is shorter than its diff:
```python
import functools

import jax
import jax.numpy as jnp
from jax import lax
from jax.experimental import pallas as pl
from jax.experimental.pallas import tpu as pltpu
from jax.sharding import PartitionSpec as P

MESH = pl.DeviceIdType.MESH
BF16 = jnp.bfloat16
F32 = jnp.float32
eps_norm = 1e-06

NZ, NY, NC, NX = 8, 4, 2, 4
GROUP = NY * NC
TOK = 128
D = 2048
CAP = 11
PIECE = 96
ROWS = GROUP * PIECE
HID = 352
NQ = 4
DQ = D // NQ
TILE = 384
PACE = 2


def nt(a, b):
    return lax.dot_general(a, b, (((1,), (1,)), ((), ())), preferred_element_type=F32)


def mm(a, b):
    return jnp.dot(a, b, preferred_element_type=F32)


def cols(q):
    return pl.ds(q * DQ, DQ)


def kernel(
    attn, ow, resid, gain, ids, wts, wgu_in, wd_in, out,
    mixed, far, nbr, far_in, nbr_in, meta_out, meta, vrow, gather, comb, gw,
    tok, ysend, yrecv, xrecv, xback, yback, zrecv, wgu, wd, acc, hidden,
    wl_sem, ws_sem, wr_sem, fs_sem, fr_sem, ns_sem, nr_sem, ms_sem, mr_sem,
    as_sem, ar_sem, ys_sem, yr_sem, xs_sem, xr_sem, bs_sem, br_sem, cs_sem, cr_sem, zs_sem, zr_sem,
):
    e = lax.axis_index("expert")
    x = lax.axis_index("tensor")
    z = e // GROUP
    y = (e // NC) % NY
    c = e % NC
    own_d = e % GROUP
    xr, xl = (x + 1) % NX, (x + NX - 1) % NX
    flip = x + 1 - 2 * (x % 2)
    mirror = NX - 1 - x
    wx = (1 - c) * mirror + c * flip
    px = (1 - c) * flip + c * mirror

    def at_z(dz):
        return (((z + dz + NZ) % NZ) * GROUP + own_d, x)

    def at_yc(j):
        return (z * GROUP + ((y + j // NC) % NY) * NC + (c + j % NC) % NC, x)

    def d_from(j):
        return ((y + NY - j // NC) % NY) * NC + (c + j % NC) % NC

    def d_to(j):
        return ((y + j // NC) % NY) * NC + (c + j % NC) % NC

    def rcopy(src, dst, send, recv, dev):
        return pltpu.make_async_remote_copy(
            src_ref=src, dst_ref=dst, send_sem=send, recv_sem=recv, device_id=dev, device_id_type=MESH
        )

    def landed(ref, sem):
        pltpu.make_async_copy(ref, ref, sem).wait()

    wloc = [
        pltpu.make_async_copy(wgu_in.at[0], wgu.at[0, pl.ds(0, HID)], wl_sem.at[0]),
        pltpu.make_async_copy(wgu_in.at[1], wgu.at[1, pl.ds(0, HID)], wl_sem.at[1]),
        pltpu.make_async_copy(wd_in, wd.at[pl.ds(0, HID)], wl_sem.at[2]),
    ]
    for copy in wloc:
        copy.start()

    barrier = pltpu.get_barrier_semaphore()
    peers = [at_z(k) for k in range(1, NZ)] + [at_yc(j) for j in range(1, GROUP)] + [(e, xr), (e, xl)]
    for dev in peers:
        pl.semaphore_signal(barrier, inc=1, device_id=dev, device_id_type=MESH)
    pl.semaphore_wait(barrier, len(peers))

    half = D // 2

    def project(owner, q):
        return mm(attn[pl.ds(pl.multiple_of(owner * TOK, TOK), TOK), :], ow[:, cols(q)])

    opposite = (x + 2) % NX
    far_copy = []
    for side in range(2):
        for q in (2 * side, 2 * side + 1):
            far[side, :, pl.ds((q % 2) * DQ, DQ)] = project(opposite, q).astype(BF16)
        far_copy.append(
            rcopy(far.at[side], far_in.at[side], fs_sem.at[side], fr_sem.at[side], (e, (xr, xl)[side]))
        )
        far_copy[-1].start()
    nbr_copy = []
    for side in range(2):
        part = 1 - side
        for q in (2 * part, 2 * part + 1):
            nbr[side, part, :, pl.ds((q % 2) * DQ, DQ)] = project((xr, xl)[side], q).astype(BF16)
        nbr_copy.append(
            rcopy(nbr.at[side, part], nbr_in.at[side, part], ns_sem.at[side, part], nr_sem.at[side, part], (e, (xr, xl)[side]))
        )
        nbr_copy[-1].start()
    for side in range(2):
        part = side
        for q in (2 * part, 2 * part + 1):
            mixed[:, cols(q)] = project((xr, xl)[side], q)
        landed(far_in.at[side], fr_sem.at[side])
        for q in (2 * part, 2 * part + 1):
            at = pl.ds((q % 2) * DQ, DQ)
            nbr[side, part, :, at] = (mixed[:, cols(q)] + far_in[side, :, at].astype(F32)).astype(BF16)
        nbr_copy.append(
            rcopy(nbr.at[side, part], nbr_in.at[side, part], ns_sem.at[side, part], nr_sem.at[side, part], (e, (xr, xl)[side]))
        )
        nbr_copy[-1].start()
    for q in range(NQ):
        mixed[:, cols(q)] = project(x, q) + resid[:, cols(q)].astype(F32)

    expert = lax.broadcasted_iota(jnp.int32, (NZ * GROUP, TOK), 0)
    holds = jnp.zeros((NZ * GROUP, TOK), F32)
    weight = jnp.zeros((NZ * GROUP, TOK), F32)
    for k in range(ids.shape[0]):
        named = expert == ids[k : k + 1, :]
        holds = holds + jnp.where(named, 1.0, 0.0)
        weight = weight + jnp.where(named, wts[k : k + 1, :], 0.0)
    before = lax.broadcasted_iota(jnp.int32, (TOK, TOK), 0) < lax.broadcasted_iota(jnp.int32, (TOK, TOK), 1)
    rank = mm(holds.astype(BF16), jnp.where(before, 1.0, 0.0).astype(BF16))
    place = jnp.where(holds > 0.5, rank + (z * CAP).astype(F32), -1.0)
    for p in range(NZ):
        meta_out[p, 0:GROUP, :] = place[p * GROUP : (p + 1) * GROUP, :]
        meta_out[p, GROUP : 2 * GROUP, :] = weight[p * GROUP : (p + 1) * GROUP, :]
    meta_copy = []
    for k in range(1, NZ):
        to = (z + k) % NZ
        meta_copy.append(rcopy(meta_out.at[to], meta.at[z], ms_sem.at[k], mr_sem.at[k], at_z(k)))
        meta_copy[-1].start()
    meta[z] = meta_out[z]

    for side in range(2):
        for part in range(2):
            landed(nbr_in.at[side, part], nr_sem.at[side, part])
            for q in (2 * part, 2 * part + 1):
                mixed[:, cols(q)] = mixed[:, cols(q)] + nbr_in[side, part, :, pl.ds((q % 2) * DQ, DQ)].astype(F32)

    wrem = [
        rcopy(wgu_in.at[0], wgu.at[0, pl.ds(HID, HID)], ws_sem.at[0], wr_sem.at[0], (e, wx)),
        rcopy(wgu_in.at[1], wgu.at[1, pl.ds(HID, HID)], ws_sem.at[1], wr_sem.at[1], (e, wx)),
        rcopy(wd_in, wd.at[pl.ds(HID, HID)], ws_sem.at[2], wr_sem.at[2], (e, wx)),
    ]
    for copy in wrem:
        copy.start()

    square = jnp.zeros((TOK, 1), F32)
    for q in range(NQ):
        part = mixed[:, cols(q)]
        square = square + jnp.sum(part * part, axis=1, keepdims=True)
    scale = lax.rsqrt(square * (1.0 / D) + eps_norm)

    def hops(q):
        return (4, 3) if q % 2 == 0 else (3, 4)

    def block(s):
        return pl.ds(pl.multiple_of(s * TOK, TOK), TOK)

    sent = {}

    def ag_send(q, side, k):
        s = (z + NZ - (k - 1)) % NZ if side == 0 else (z + k - 1) % NZ
        ref = tok.at[q, block(s)]
        copy = rcopy(ref, ref, as_sem.at[q, side, k - 1], ar_sem.at[q, side, k - 1], at_z(1 if side == 0 else -1))
        copy.start()
        sent.setdefault(("ag", q), []).append(copy)

    def ag_start(q):
        tok[q, block(z), :] = (mixed[:, cols(q)] * scale * gain[:, cols(q)]).astype(BF16)
        for side in range(2):
            ag_send(q, side, 1)

    def ag_step(q, k):
        for side in range(2):
            if k > hops(q)[side]:
                continue
            s = (z + NZ - k) % NZ if side == 0 else (z + k) % NZ
            landed(tok.at[q, block(s)], ar_sem.at[q, side, k - 1])
            if k < hops(q)[side]:
                ag_send(q, side, k + 1)

    def piece(d):
        return pl.ds(pl.multiple_of(d * PIECE, 32), PIECE)

    def gather_step(q):
        def one(i, _):
            at = pl.ds(pl.multiple_of(i * TILE, TILE), TILE)
            ysend[q, at, :] = mm(gather[at, :], tok[q]).astype(BF16)
            return 0

        lax.fori_loop(0, ROWS // TILE, one, 0)
        for j in range(GROUP - 1, 0, -1):
            copy = rcopy(
                ysend.at[q, piece(d_to(j))], yrecv.at[q, piece(own_d)], ys_sem.at[q, j], yr_sem.at[q, j], at_yc(j)
            )
            copy.start()
            sent.setdefault(("y", q), []).append(copy)
        yrecv[q, piece(own_d), :] = ysend[q, piece(own_d), :]

    def share_step(q):
        for j in range(1, GROUP):
            landed(yrecv.at[q, piece(d_from(j))], yr_sem.at[q, j])
        copy = rcopy(yrecv.at[q], xrecv.at[q], xs_sem.at[q], xr_sem.at[q], (e, px))
        copy.start()
        sent[("x", q)] = [copy]

    def hidden_step(q, who):
        if q == 0 and who == 0:
            for copy in wloc:
                copy.wait()
            for i in range(2):
                landed(wgu.at[i, pl.ds(HID, HID)], wr_sem.at[i])
            landed(wd.at[pl.ds(HID, HID)], wr_sem.at[2])
        if who == 1:
            landed(xrecv.at[q], xr_sem.at[q])
        rows = (yrecv, xrecv)[who]

        def one(i, _):
            at = pl.ds(pl.multiple_of(i * TILE, TILE), TILE)
            to = pl.ds(pl.multiple_of(i * TILE + who * ROWS, TILE), TILE)
            lhs = rows[q, at, :]
            gate = nt(lhs, wgu[0, :, cols(q)])
            up = nt(lhs, wgu[1, :, cols(q)])
            if q > 0:
                gate = gate + acc[0, to, :]
                up = up + acc[1, to, :]
            if q < NQ - 1:
                acc[0, to, :] = gate
                acc[1, to, :] = up
            else:
                hidden[to, :] = (gate / (1.0 + jnp.exp(-gate)) * up).astype(BF16)
            return 0

        lax.fori_loop(0, ROWS // TILE, one, 0)

    def masks():
        for k in range(1, NZ):
            landed(meta.at[(z + NZ - k) % NZ], mr_sem.at[k])
        slot = lax.broadcasted_iota(jnp.int32, (PIECE, TOK), 0).astype(F32)
        eye = jnp.where(
            lax.broadcasted_iota(jnp.int32, (TOK, TOK), 0) == lax.broadcasted_iota(jnp.int32, (TOK, TOK), 1), 1.0, 0.0
        ).astype(BF16)
        for s in range(NZ):
            for d in range(GROUP):
                taken = slot == meta[s, d : d + 1, :]
                gather[d * PIECE : (d + 1) * PIECE, s * TOK : (s + 1) * TOK] = jnp.where(taken, 1.0, 0.0).astype(BF16)
                gw[d * PIECE : (d + 1) * PIECE, :] = jnp.where(
                    taken, meta[s, GROUP + d : GROUP + d + 1, :], 0.0
                ).astype(BF16)
            comb[s * TOK : (s + 1) * TOK, :] = nt(eye, gw[...]).astype(BF16)

    tasks = []
    for q in range(NQ):
        t = q * PACE
        tasks.append((t, 0, functools.partial(ag_start, q)))
        for k in range(1, 5):
            tasks.append((t + k, 1, functools.partial(ag_step, q, k)))
        tasks.append((t + 4, 2, functools.partial(gather_step, q)))
        tasks.append((t + 7, 3, functools.partial(share_step, q)))
        tasks.append((t + 7, 4, functools.partial(hidden_step, q, 0)))
        tasks.append((t + 10, 5, functools.partial(hidden_step, q, 1)))
    tasks.append((0, 9, masks))
    for task in sorted(tasks, key=lambda task: task[:2]):
        task[2]()

    def down_step(q):
        for copy in sent[("x", q)]:
            copy.wait_send()

        def one(who):
            def body(i, _):
                at = pl.ds(pl.multiple_of(i * TILE, TILE), TILE)
                of = pl.ds(pl.multiple_of(i * TILE + who * ROWS, TILE), TILE)
                (yrecv, xrecv)[who][q, at, :] = mm(hidden[of, :], wd[:, cols(q)]).astype(BF16)
                return 0

            lax.fori_loop(0, ROWS // TILE, body, 0)

        one(1)
        copy = rcopy(xrecv.at[q], xback.at[q], bs_sem.at[q], br_sem.at[q], (e, px))
        copy.start()
        sent[("b", q)] = [copy]
        one(0)

    def sum_step(q):
        landed(xback.at[q], br_sem.at[q])
        for copy in sent[("y", q)]:
            copy.wait_send()
        ysend[q] = (yrecv[q].astype(F32) + xback[q].astype(F32)).astype(BF16)
        for j in range(GROUP - 1, 0, -1):
            copy = rcopy(
                ysend.at[q, piece(d_to(j))], yback.at[q, piece(own_d)], cs_sem.at[q, j], cr_sem.at[q, j], at_yc(j)
            )
            copy.start()
            sent.setdefault(("c", q), []).append(copy)
        yback[q, piece(own_d), :] = ysend[q, piece(own_d), :]

    def rs_send(q, side, j):
        far_hops = hops(q)[side]
        k = far_hops + 1 - j
        s = (z + k) % NZ if side == 0 else (z + NZ - k) % NZ
        copy = rcopy(
            tok.at[q, block(s)], zrecv.at[q, side, j - 1], zs_sem.at[q, side, j - 1], zr_sem.at[q, side, j - 1],
            at_z(1 if side == 0 else -1),
        )
        copy.start()
        sent.setdefault(("z", q), []).append(copy)

    def combine_step(q):
        for j in range(1, GROUP):
            landed(yback.at[q, piece(d_from(j))], cr_sem.at[q, j])
        for copy in sent[("ag", q)]:
            copy.wait_send()

        def one(i, _):
            at = pl.ds(pl.multiple_of(i * 256, 256), 256)
            tok[q, at, :] = mm(comb[at, :], yback[q]).astype(BF16)
            return 0

        lax.fori_loop(0, NZ * TOK // 256, one, 0)
        for side in range(2):
            rs_send(q, side, 1)

    def rs_step(q, j):
        for side in range(2):
            far_hops = hops(q)[side]
            if j > far_hops:
                continue
            landed(zrecv.at[q, side, j - 1], zr_sem.at[q, side, j - 1])
            if j == far_hops:
                mixed[:, cols(q)] = mixed[:, cols(q)] + zrecv[q, side, j - 1].astype(F32)
                continue
            k = far_hops - j
            s = (z + k) % NZ if side == 0 else (z + NZ - k) % NZ
            tok[q, block(s), :] = (tok[q, block(s), :].astype(F32) + zrecv[q, side, j - 1].astype(F32)).astype(BF16)
            rs_send(q, side, j + 1)

    def finish(q):
        out[:, cols(q)] = (mixed[:, cols(q)] + tok[q, block(z), :].astype(F32)).astype(BF16)

    tasks = []
    for q in range(NQ):
        t = q * PACE
        tasks.append((q, 0, functools.partial(down_step, q)))
        tasks.append((t + 4, 1, functools.partial(sum_step, q)))
        tasks.append((t + 7, 2, functools.partial(combine_step, q)))
        for j in range(1, 5):
            tasks.append((t + 7 + j, 3, functools.partial(rs_step, q, j)))
        tasks.append((t + 11, 4, functools.partial(finish, q)))
    for task in sorted(tasks, key=lambda task: task[:2]):
        task[2]()

    for copy in far_copy + nbr_copy + meta_copy + wrem:
        copy.wait_send()
    for q in range(NQ):
        for kind in ("b", "c", "z"):
            for copy in sent[(kind, q)]:
                copy.wait_send()


def on_device(
    attn_heads, o_weight, resid, norm_gain, expert_ids, combine_weights, w_gate_up, w_down
):
    vmem = pl.BlockSpec(memory_space=pltpu.VMEM)
    hbm = pl.BlockSpec(memory_space=pl.ANY)
    dma = pltpu.SemaphoreType.DMA
    return pl.pallas_call(
        kernel,
        out_shape=jax.ShapeDtypeStruct((TOK, D), BF16),
        in_specs=[vmem] * 6 + [hbm] * 2,
        out_specs=vmem,
        scratch_shapes=[
            pltpu.VMEM((TOK, D), F32),
            pltpu.VMEM((2, TOK, D // 2), BF16),
            pltpu.VMEM((2, 2, TOK, D // 2), BF16),
            pltpu.VMEM((2, TOK, D // 2), BF16),
            pltpu.VMEM((2, 2, TOK, D // 2), BF16),
            pltpu.VMEM((NZ, 2 * GROUP, TOK), F32),
            pltpu.VMEM((NZ, 2 * GROUP, TOK), F32),
            pltpu.VMEM((8, TOK), F32),
            pltpu.VMEM((ROWS, NZ * TOK), BF16),
            pltpu.VMEM((NZ * TOK, ROWS), BF16),
            pltpu.VMEM((ROWS, TOK), BF16),
            pltpu.VMEM((NQ, NZ * TOK, DQ), BF16),
            pltpu.VMEM((NQ, ROWS, DQ), BF16),
            pltpu.VMEM((NQ, ROWS, DQ), BF16),
            pltpu.VMEM((NQ, ROWS, DQ), BF16),
            pltpu.VMEM((NQ, ROWS, DQ), BF16),
            pltpu.VMEM((NQ, ROWS, DQ), BF16),
            pltpu.VMEM((NQ, 2, 4, TOK, DQ), BF16),
            pltpu.VMEM((2, 2 * HID, D), BF16),
            pltpu.VMEM((2 * HID, D), BF16),
            pltpu.VMEM((2, 2 * ROWS, 2 * HID), F32),
            pltpu.VMEM((2 * ROWS, 2 * HID), BF16),
            dma((3,)), dma((3,)), dma((3,)),
            dma((2,)), dma((2,)), dma((2, 2)), dma((2, 2)), dma((NZ,)), dma((NZ,)),
            dma((NQ, 2, 4)), dma((NQ, 2, 4)), dma((NQ, GROUP)), dma((NQ, GROUP)), dma((NQ,)), dma((NQ,)),
            dma((NQ,)), dma((NQ,)), dma((NQ, GROUP)), dma((NQ, GROUP)), dma((NQ, 2, 4)), dma((NQ, 2, 4)),
        ],
        compiler_params=pltpu.CompilerParams(
            collective_id=0, has_side_effects=True, vmem_limit_bytes=60 * 2**20
        ),
        cost_estimate=pl.CostEstimate(flops=16 * 10**9, bytes_accessed=10**7, transcendentals=10**6),
    )(
        attn_heads, o_weight, resid, norm_gain[None, :], expert_ids.T, combine_weights.T,
        jnp.swapaxes(w_gate_up[0], 1, 2), w_down[0],
    )


def solution(mesh):
    in_specs = (
        P("expert", "tensor"),
        P("tensor", None),
        P(("expert", "tensor"), None),
        P(),
        P(("expert", "tensor"), None),
        P(("expert", "tensor"), None),
        P("expert", None, None, "tensor"),
        P("expert", "tensor", None),
    )
    out_specs = P(("expert", "tensor"), None)
    return jax.shard_map(
        on_device, mesh=mesh, in_specs=in_specs, out_specs=out_specs, check_vma=False
    )
```

time: 376 us -> 208 us (0.55)
  Pallas kernels: 0 us -> 206 us
  waiting for transfers between devices: 168 us -> 0 us
  blocking collectives: 107 us -> 0 us
  matrix products: 47.1 us -> 0 us
  local copies, waits for them, and re-layouts: 27.8 us -> 1.88 us
  between operations: 13.2 us -> 0.01 us
  starting transfers between devices: 10.9 us -> 0 us
    pallas_call x0 -> x1, Pallas kernels: none -> 206 us  [on_device(): pl.pallas_call(kernel, out_shape=jax.ShapeDtypeStruct((TOK, D), BF16), in...]
    all_to_all x1 -> x0, blocking collectives: 107 us -> none  [on_device(): lax.all_to_all(outgoing.reshape(num_experts, capacity, width), 'expert',...]
    all_to_all x1 -> x0, waiting for transfers between devices: 96.2 us -> none  [on_device(): lax.all_to_all(total.reshape(num_experts, capacity, width), 'expert', spl...]
    dot_general x7 -> x0, matrix products: 47.1 us -> none  [the longest x1 17.3 us: on_device(): jnp.dot(hidden, down_all, preferred_element_type=jnp.float32)]
    all_gather x2 -> x0, waiting for transfers between devices: 38.4 us -> none  [the longest x1 38.4 us: on_device(): down_all = lax.all_gather(w_down[0], 'tensor', axis=0, tiled=True)]
    reduce_scatter x1 -> x0, waiting for transfers between devices: 32.1 us -> none  [on_device(): lax.psum_scatter(partial, 'tensor', scatter_dimension=0, tiled=True)]
    reshape x3 -> x0, local copies, waits for them, and re-layouts: 14.3 us -> none  [the longest x1 4.81 us: on_device(): received = lax.all_to_all(outgoing.reshape(num_experts, capacity, width),...]
    slice x1 -> x0, local copies, waits for them, and re-layouts: 11.6 us -> none  [on_device(): gate_up_all[:, 1].reshape(-1, width)]
  transfers between devices with their start and end apart: 4 -> 0, of which waited for: 3 -> 0; matrix products, arithmetic and copies ran while one was open for 10% -> 0% of each run, Pallas kernels for 0% -> 0%
where the time goes in v2:
time: 208 us
  Pallas kernels  206 us (99%)
    pallas_call x1, Pallas kernels, on_device(): pl.pallas_call(kernel, out_shape=jax.ShapeDtypeStruct((TOK, D), BF16), in...  206 us

profile of v2, /device:TPU:2, one launch (start us, length us, event | category | flops | bytes accessed | tf_op | source)
XLA Modules:
  0.0 207.6 jit_solution(5762716761959024616)
XLA Ops:
  0.0 205.7 %shard_map.82 = bf16[128,2048]{1,0:T(8,128)(2,1)} custom-call(bf16[512,512]{1,0:T(8,128)(2,1)} %attn.1, bf16[512,2048]{1,0:T(8,128)(2,1)} %ow.1, bf16[128,2048]{1,0:T(8,128)(2,1)} %resid.1, f32[1,2048]{1,0:T(1,128)} %bitcast.9, s32[4,128]{1,0:T(4,128)} %bitcast.10, f32[4,128]{1,0:T(4,128)} %bitcast.11, bf16[2,352,2048]{2,1,0:T(8,128)(2,1)} %bitcast.7, ...), custom_call_target="tpu_custom_call" | custom-call | flops 16000000000 | bytes 10000000 | tf_op jit(solution)/shard_map/pallas_call | solution.py:386
  205.7 1.9 copy.10

commit v3 on v2

--- a/solution.py
+++ b/solution.py
@@ -20,10 +20,13 @@
 PIECE = 96
 ROWS = GROUP * PIECE
 HID = 352
-NQ = 4
+NQ = 8
 DQ = D // NQ
 TILE = 384
-PACE = 2
+AHEAD = 2
+YLAG = 2
+XT, YT, ZT = 4, 5, 3
+PACE = 1
 
 
 def nt(a, b):
@@ -34,12 +37,20 @@
     return jnp.dot(a, b, preferred_element_type=F32)
 
 
+PQ = 512
+
+
+def pcols(q):
+    return pl.ds(q * PQ, PQ)
+
+
 def cols(q):
     return pl.ds(q * DQ, DQ)
 
 
 def kernel(
-    attn, ow, resid, gain, ids, wts, wgu_in, wd_in, out,
+    attn_in, ow_in, resid_in, gain, ids, wts, wgu_in, wd_in, out,
+    attn, ow, resid, in_sem,
     mixed, far, nbr, far_in, nbr_in, meta_out, meta, vrow, gather, comb, gw,
     tok, ysend, yrecv, xrecv, xback, yback, zrecv, wgu, wd, acc, hidden,
     wl_sem, ws_sem, wr_sem, fs_sem, fr_sem, ns_sem, nr_sem, ms_sem, mr_sem,
@@ -77,12 +88,17 @@
     def landed(ref, sem):
         pltpu.make_async_copy(ref, ref, sem).wait()
 
+    inputs = [
+        pltpu.make_async_copy(attn_in, attn, in_sem.at[0]),
+        pltpu.make_async_copy(ow_in, ow, in_sem.at[1]),
+        pltpu.make_async_copy(resid_in, resid, in_sem.at[2]),
+    ]
     wloc = [
         pltpu.make_async_copy(wgu_in.at[0], wgu.at[0, pl.ds(0, HID)], wl_sem.at[0]),
         pltpu.make_async_copy(wgu_in.at[1], wgu.at[1, pl.ds(0, HID)], wl_sem.at[1]),
         pltpu.make_async_copy(wd_in, wd.at[pl.ds(0, HID)], wl_sem.at[2]),
     ]
-    for copy in wloc:
+    for copy in inputs + wloc:
         copy.start()
 
     barrier = pltpu.get_barrier_semaphore()
@@ -91,16 +107,17 @@
         pl.semaphore_signal(barrier, inc=1, device_id=dev, device_id_type=MESH)
     pl.semaphore_wait(barrier, len(peers))
 
-    half = D // 2
+    inputs[0].wait()
+    inputs[1].wait()
 
     def project(owner, q):
-        return mm(attn[pl.ds(pl.multiple_of(owner * TOK, TOK), TOK), :], ow[:, cols(q)])
+        return mm(attn[pl.ds(pl.multiple_of(owner * TOK, TOK), TOK), :], ow[:, pcols(q)])
 
     opposite = (x + 2) % NX
     far_copy = []
     for side in range(2):
         for q in (2 * side, 2 * side + 1):
-            far[side, :, pl.ds((q % 2) * DQ, DQ)] = project(opposite, q).astype(BF16)
+            far[side, :, pl.ds((q % 2) * PQ, PQ)] = project(opposite, q).astype(BF16)
         far_copy.append(
             rcopy(far.at[side], far_in.at[side], fs_sem.at[side], fr_sem.at[side], (e, (xr, xl)[side]))
         )
@@ -109,7 +126,7 @@
     for side in range(2):
         part = 1 - side
         for q in (2 * part, 2 * part + 1):
-            nbr[side, part, :, pl.ds((q % 2) * DQ, DQ)] = project((xr, xl)[side], q).astype(BF16)
+            nbr[side, part, :, pl.ds((q % 2) * PQ, PQ)] = project((xr, xl)[side], q).astype(BF16)
         nbr_copy.append(
             rcopy(nbr.at[side, part], nbr_in.at[side, part], ns_sem.at[side, part], nr_sem.at[side, part], (e, (xr, xl)[side]))
         )
@@ -117,17 +134,26 @@
     for side in range(2):
         part = side
         for q in (2 * part, 2 * part + 1):
-            mixed[:, cols(q)] = project((xr, xl)[side], q)
+            mixed[:, pcols(q)] = project((xr, xl)[side], q)
         landed(far_in.at[side], fr_sem.at[side])
         for q in (2 * part, 2 * part + 1):
-            at = pl.ds((q % 2) * DQ, DQ)
-            nbr[side, part, :, at] = (mixed[:, cols(q)] + far_in[side, :, at].astype(F32)).astype(BF16)
+            at = pl.ds((q % 2) * PQ, PQ)
+            nbr[side, part, :, at] = (mixed[:, pcols(q)] + far_in[side, :, at].astype(F32)).astype(BF16)
         nbr_copy.append(
             rcopy(nbr.at[side, part], nbr_in.at[side, part], ns_sem.at[side, part], nr_sem.at[side, part], (e, (xr, xl)[side]))
         )
         nbr_copy[-1].start()
-    for q in range(NQ):
-        mixed[:, cols(q)] = project(x, q) + resid[:, cols(q)].astype(F32)
+    wrem = [
+        rcopy(wgu_in.at[0], wgu.at[0, pl.ds(HID, HID)], ws_sem.at[0], wr_sem.at[0], (e, wx)),
+        rcopy(wgu_in.at[1], wgu.at[1, pl.ds(HID, HID)], ws_sem.at[1], wr_sem.at[1], (e, wx)),
+        rcopy(wd_in, wd.at[pl.ds(HID, HID)], ws_sem.at[2], wr_sem.at[2], (e, wx)),
+    ]
+    for copy in wrem:
+        copy.start()
+
+    inputs[2].wait()
+    for q in range(4):
+        mixed[:, pcols(q)] = project(x, q) + resid[:, pcols(q)].astype(F32)
 
     expert = lax.broadcasted_iota(jnp.int32, (NZ * GROUP, TOK), 0)
     holds = jnp.zeros((NZ * GROUP, TOK), F32)
@@ -153,15 +179,7 @@
         for part in range(2):
             landed(nbr_in.at[side, part], nr_sem.at[side, part])
             for q in (2 * part, 2 * part + 1):
-                mixed[:, cols(q)] = mixed[:, cols(q)] + nbr_in[side, part, :, pl.ds((q % 2) * DQ, DQ)].astype(F32)
-
-    wrem = [
-        rcopy(wgu_in.at[0], wgu.at[0, pl.ds(HID, HID)], ws_sem.at[0], wr_sem.at[0], (e, wx)),
-        rcopy(wgu_in.at[1], wgu.at[1, pl.ds(HID, HID)], ws_sem.at[1], wr_sem.at[1], (e, wx)),
-        rcopy(wd_in, wd.at[pl.ds(HID, HID)], ws_sem.at[2], wr_sem.at[2], (e, wx)),
-    ]
-    for copy in wrem:
-        copy.start()
+                mixed[:, pcols(q)] = mixed[:, pcols(q)] + nbr_in[side, part, :, pl.ds((q % 2) * PQ, PQ)].astype(F32)
 
     square = jnp.zeros((TOK, 1), F32)
     for q in range(NQ):
@@ -268,41 +286,43 @@
                 ).astype(BF16)
             comb[s * TOK : (s + 1) * TOK, :] = nt(eye, gw[...]).astype(BF16)
 
-    tasks = []
+    tasks = [(0, 9, masks)]
     for q in range(NQ):
         t = q * PACE
         tasks.append((t, 0, functools.partial(ag_start, q)))
         for k in range(1, 5):
             tasks.append((t + k, 1, functools.partial(ag_step, q, k)))
         tasks.append((t + 4, 2, functools.partial(gather_step, q)))
-        tasks.append((t + 7, 3, functools.partial(share_step, q)))
-        tasks.append((t + 7, 4, functools.partial(hidden_step, q, 0)))
-        tasks.append((t + 10, 5, functools.partial(hidden_step, q, 1)))
-    tasks.append((0, 9, masks))
+        tasks.append((t + 4 + YLAG, 3, functools.partial(share_step, q)))
+        tasks.append((100 + q, 4, functools.partial(hidden_step, q, 0)))
+        tasks.append((200 + q, 5, functools.partial(hidden_step, q, 1)))
     for task in sorted(tasks, key=lambda task: task[:2]):
         task[2]()
 
-    def down_step(q):
+    def down_step(q, who):
         for copy in sent[("x", q)]:
             copy.wait_send()
-
-        def one(who):
-            def body(i, _):
-                at = pl.ds(pl.multiple_of(i * TILE, TILE), TILE)
-                of = pl.ds(pl.multiple_of(i * TILE + who * ROWS, TILE), TILE)
-                (yrecv, xrecv)[who][q, at, :] = mm(hidden[of, :], wd[:, cols(q)]).astype(BF16)
-                return 0
-
-            lax.fori_loop(0, ROWS // TILE, body, 0)
-
-        one(1)
-        copy = rcopy(xrecv.at[q], xback.at[q], bs_sem.at[q], br_sem.at[q], (e, px))
-        copy.start()
-        sent[("b", q)] = [copy]
-        one(0)
+        sent[("x", q)] = []
+
+        def body(i, _):
+            at = pl.ds(pl.multiple_of(i * TILE, TILE), TILE)
+            of = pl.ds(pl.multiple_of(i * TILE + who * ROWS, TILE), TILE)
+            (yrecv, xrecv)[who][q, at, :] = mm(hidden[of, :], wd[:, cols(q)]).astype(BF16)
+            return 0
+
+        lax.fori_loop(0, ROWS // TILE, body, 0)
+        if who == 1 and q < AHEAD:
+            give_back(q)
+
+    def give_back(q):
+        if q < NQ:
+            copy = rcopy(xrecv.at[q], xback.at[q], bs_sem.at[q], br_sem.at[q], (e, px))
+            copy.start()
+            sent[("b", q)] = [copy]
 
     def sum_step(q):
         landed(xback.at[q], br_sem.at[q])
+        give_back(q + AHEAD)
         for copy in sent[("y", q)]:
             copy.wait_send()
         ysend[q] = (yrecv[q].astype(F32) + xback[q].astype(F32)).astype(BF16)
@@ -359,13 +379,14 @@
 
     tasks = []
     for q in range(NQ):
-        t = q * PACE
-        tasks.append((q, 0, functools.partial(down_step, q)))
-        tasks.append((t + 4, 1, functools.partial(sum_step, q)))
-        tasks.append((t + 7, 2, functools.partial(combine_step, q)))
+        t = (q + 1) * XT
+        tasks.append((-200 + q, 0, functools.partial(down_step, q, 1)))
+        tasks.append((-100 + q, 0, functools.partial(down_step, q, 0)))
+        tasks.append((t, 1, functools.partial(sum_step, q)))
+        tasks.append((t + YT, 2, functools.partial(combine_step, q)))
         for j in range(1, 5):
-            tasks.append((t + 7 + j, 3, functools.partial(rs_step, q, j)))
-        tasks.append((t + 11, 4, functools.partial(finish, q)))
+            tasks.append((t + YT + j * ZT, 3, functools.partial(rs_step, q, j)))
+        tasks.append((t + YT + 4 * ZT, 4, functools.partial(finish, q)))
     for task in sorted(tasks, key=lambda task: task[:2]):
         task[2]()
 
@@ -386,9 +407,13 @@
     return pl.pallas_call(
         kernel,
         out_shape=jax.ShapeDtypeStruct((TOK, D), BF16),
-        in_specs=[vmem] * 6 + [hbm] * 2,
+        in_specs=[hbm] * 3 + [vmem] * 3 + [hbm] * 2,
         out_specs=vmem,
         scratch_shapes=[
+            pltpu.VMEM((4 * TOK, D // NX), BF16),
+            pltpu.VMEM((D // NX, D), BF16),
+            pltpu.VMEM((TOK, D), BF16),
+            dma((3,)),
             pltpu.VMEM((TOK, D), F32),
             pltpu.VMEM((2, TOK, D // 2), BF16),
             pltpu.VMEM((2, 2, TOK, D // 2), BF16),

time: 208 us -> 191 us (0.918)
  Pallas kernels: 206 us -> 189 us
    pallas_call x1, Pallas kernels: 206 us -> 189 us  [on_device(): pl.pallas_call(kernel, out_shape=jax.ShapeDtypeStruct((TOK, D), BF16), in...]
where the time goes in v3:
time: 191 us
  Pallas kernels  189 us (99%)
    pallas_call x1, Pallas kernels, on_device(): pl.pallas_call(kernel, out_shape=jax.ShapeDtypeStruct((TOK, D), BF16), in...  189 us

profile of v3, /device:TPU:2, one launch (start us, length us, event | category | flops | bytes accessed | tf_op | source)
XLA Modules:
  0.0 190.9 jit_solution(6286482060191743769)
XLA Ops:
  0.0 189.0 %shard_map.82 = bf16[128,2048]{1,0:T(8,128)(2,1)} custom-call(bf16[512,512]{1,0:T(8,128)(2,1)} %attn_in.1, bf16[512,2048]{1,0:T(8,128)(2,1)} %ow_in.1, bf16[128,2048]{1,0:T(8,128)(2,1)} %resid_in.1, f32[1,2048]{1,0:T(1,128)} %bitcast.9, s32[4,128]{1,0:T(4,128)} %bitcast.10, f32[4,128]{1,0:T(4,128)} %bitcast.11, bf16[2,352,2048]{2,1,0:T(8,128)(2,1)} %bitcast.7, ...), custom_call_target="tpu_custom_call" | custom-call | flops 16000000000 | bytes 10000000 | tf_op jit(solution)/shard_map/pallas_call | solution.py:407
  189.0 1.9 copy.10

commit v4 on v3

--- a/solution.py
+++ b/solution.py
@@ -23,9 +23,10 @@
 NQ = 8
 DQ = D // NQ
 TILE = 384
-AHEAD = 2
 YLAG = 2
 XT, YT, ZT = 4, 5, 3
+THEIR = (0, 0.5, 1, 2, 3, 3.5, 5, 6)
+OUR = (1.5, 2.5, 5.5, 6.5, 9, 9.5, 13, 13.5)
 PACE = 1
 
 
@@ -311,18 +312,13 @@
             return 0
 
         lax.fori_loop(0, ROWS // TILE, body, 0)
-        if who == 1 and q < AHEAD:
-            give_back(q)
-
-    def give_back(q):
-        if q < NQ:
+        if who == 1:
             copy = rcopy(xrecv.at[q], xback.at[q], bs_sem.at[q], br_sem.at[q], (e, px))
             copy.start()
             sent[("b", q)] = [copy]
 
     def sum_step(q):
         landed(xback.at[q], br_sem.at[q])
-        give_back(q + AHEAD)
         for copy in sent[("y", q)]:
             copy.wait_send()
         ysend[q] = (yrecv[q].astype(F32) + xback[q].astype(F32)).astype(BF16)
@@ -380,8 +376,8 @@
     tasks = []
     for q in range(NQ):
         t = (q + 1) * XT
-        tasks.append((-200 + q, 0, functools.partial(down_step, q, 1)))
-        tasks.append((-100 + q, 0, functools.partial(down_step, q, 0)))
+        tasks.append((OUR[q], 0, functools.partial(down_step, q, 0)))
+        tasks.append((THEIR[q], 0, functools.partial(down_step, q, 1)))
         tasks.append((t, 1, functools.partial(sum_step, q)))
         tasks.append((t + YT, 2, functools.partial(combine_step, q)))
         for j in range(1, 5):

time: 191 us -> 187 us (0.979)
  Pallas kernels: 189 us -> 185 us
    pallas_call x1, Pallas kernels: 189 us -> 185 us  [on_device(): pl.pallas_call(kernel, out_shape=jax.ShapeDtypeStruct((TOK, D), BF16), in...]
where the time goes in v4:
time: 187 us
  Pallas kernels  185 us (99%)
  local copies, waits for them, and re-layouts  1.88 us (1%)
    pallas_call x1, Pallas kernels, on_device(): pl.pallas_call(kernel, out_shape=jax.ShapeDtypeStruct((TOK, D), BF16), in...  185 us

profile of v4, /device:TPU:2, one launch (start us, length us, event | category | flops | bytes accessed | tf_op | source)
XLA Modules:
  0.0 187.1 jit_solution(3502652736363342969)
XLA Ops:
  0.0 185.2 %shard_map.82 = bf16[128,2048]{1,0:T(8,128)(2,1)} custom-call(bf16[512,512]{1,0:T(8,128)(2,1)} %attn_in.1, bf16[512,2048]{1,0:T(8,128)(2,1)} %ow_in.1, bf16[128,2048]{1,0:T(8,128)(2,1)} %resid_in.1, f32[1,2048]{1,0:T(1,128)} %bitcast.9, s32[4,128]{1,0:T(4,128)} %bitcast.10, f32[4,128]{1,0:T(4,128)} %bitcast.11, bf16[2,352,2048]{2,1,0:T(8,128)(2,1)} %bitcast.7, ...), custom_call_target="tpu_custom_call" | custom-call | flops 16000000000 | bytes 10000000 | tf_op jit(solution)/shard_map/pallas_call | solution.py:403
  185.2 1.9 %copy.10 = bf16[128,2048]{1,0:T(8,128)(2,1)} copy(bf16[128,2048]{1,0:T(8,128)(2,1)} %shard_map.82) | data formatting | bytes 1048576

commit v5 on v4

--- a/solution.py
+++ b/solution.py
@@ -24,7 +24,7 @@
 DQ = D // NQ
 TILE = 384
 YLAG = 2
-XT, YT, ZT = 4, 5, 3
+XT, YT, ZT, ZQ = 4.6, 7, 3.5, 5.5
 THEIR = (0, 0.5, 1, 2, 3, 3.5, 5, 6)
 OUR = (1.5, 2.5, 5.5, 6.5, 9, 9.5, 13, 13.5)
 PACE = 1
@@ -295,8 +295,8 @@
             tasks.append((t + k, 1, functools.partial(ag_step, q, k)))
         tasks.append((t + 4, 2, functools.partial(gather_step, q)))
         tasks.append((t + 4 + YLAG, 3, functools.partial(share_step, q)))
-        tasks.append((100 + q, 4, functools.partial(hidden_step, q, 0)))
-        tasks.append((200 + q, 5, functools.partial(hidden_step, q, 1)))
+        tasks.append((PACE * (NQ + 3) + 0.5 if q < 3 else 100 + q, 4 + q / NQ, functools.partial(hidden_step, q, 0)))
+        tasks.append((200 + q, 6, functools.partial(hidden_step, q, 1)))
     for task in sorted(tasks, key=lambda task: task[:2]):
         task[2]()
 
@@ -381,8 +381,8 @@
         tasks.append((t, 1, functools.partial(sum_step, q)))
         tasks.append((t + YT, 2, functools.partial(combine_step, q)))
         for j in range(1, 5):
-            tasks.append((t + YT + j * ZT, 3, functools.partial(rs_step, q, j)))
-        tasks.append((t + YT + 4 * ZT, 4, functools.partial(finish, q)))
+            tasks.append((XT + YT + q * ZQ + j * ZT, 3, functools.partial(rs_step, q, j)))
+        tasks.append((XT + YT + q * ZQ + 4 * ZT, 4, functools.partial(finish, q)))
     for task in sorted(tasks, key=lambda task: task[:2]):
         task[2]()
 

time: 187 us -> 192 us (1.027)
  Pallas kernels: 185 us -> 190 us
    pallas_call x1, Pallas kernels: 185 us -> 190 us  [on_device(): pl.pallas_call(kernel, out_shape=jax.ShapeDtypeStruct((TOK, D), BF16), in...]
where the time goes in v5:
time: 192 us; the launch traced here: 191 us
  Pallas kernels  190 us (99%)
    pallas_call x1, Pallas kernels, on_device(): pl.pallas_call(kernel, out_shape=jax.ShapeDtypeStruct((TOK, D), BF16), in...  190 us

profile of v5, /device:TPU:2, one launch (start us, length us, event | category | flops | bytes accessed | tf_op | source)
XLA Modules:
  0.0 191.4 jit_solution(1616447880242962217)
XLA Ops:
  0.0 189.5 %shard_map.82 = bf16[128,2048]{1,0:T(8,128)(2,1)} custom-call(bf16[512,512]{1,0:T(8,128)(2,1)} %attn_in.1, bf16[512,2048]{1,0:T(8,128)(2,1)} %ow_in.1, bf16[128,2048]{1,0:T(8,128)(2,1)} %resid_in.1, f32[1,2048]{1,0:T(1,128)} %bitcast.9, s32[4,128]{1,0:T(4,128)} %bitcast.10, f32[4,128]{1,0:T(4,128)} %bitcast.11, bf16[2,352,2048]{2,1,0:T(8,128)(2,1)} %bitcast.7, ...), custom_call_target="tpu_custom_call" | custom-call | flops 16000000000 | bytes 10000000 | tf_op jit(solution)/shard_map/pallas_call | solution.py:403
  189.5 1.9 copy.10

commit v6 on v4

--- a/solution.py
+++ b/solution.py
@@ -24,7 +24,7 @@
 DQ = D // NQ
 TILE = 384
 YLAG = 2
-XT, YT, ZT = 4, 5, 3
+XT, YT, ZT = 4, 4.5, 2
 THEIR = (0, 0.5, 1, 2, 3, 3.5, 5, 6)
 OUR = (1.5, 2.5, 5.5, 6.5, 9, 9.5, 13, 13.5)
 PACE = 1

time: 187 us -> 207 us (1.11)
  Pallas kernels: 185 us -> 205 us
    pallas_call x1, Pallas kernels: 185 us -> 205 us  [on_device(): pl.pallas_call(kernel, out_shape=jax.ShapeDtypeStruct((TOK, D), BF16), in...]
where the time goes in v6:
time: 207 us
  Pallas kernels  205 us (99%)
    pallas_call x1, Pallas kernels, on_device(): pl.pallas_call(kernel, out_shape=jax.ShapeDtypeStruct((TOK, D), BF16), in...  205 us

profile of v6, /device:TPU:2, one launch (start us, length us, event | category | flops | bytes accessed | tf_op | source)
XLA Modules:
  0.0 206.7 jit_solution(14153775705102945754)
XLA Ops:
  0.0 204.9 %shard_map.82 = bf16[128,2048]{1,0:T(8,128)(2,1)} custom-call(bf16[512,512]{1,0:T(8,128)(2,1)} %attn_in.1, bf16[512,2048]{1,0:T(8,128)(2,1)} %ow_in.1, bf16[128,2048]{1,0:T(8,128)(2,1)} %resid_in.1, f32[1,2048]{1,0:T(1,128)} %bitcast.9, s32[4,128]{1,0:T(4,128)} %bitcast.10, f32[4,128]{1,0:T(4,128)} %bitcast.11, bf16[2,352,2048]{2,1,0:T(8,128)(2,1)} %bitcast.7, ...), custom_call_target="tpu_custom_call" | custom-call | flops 16000000000 | bytes 10000000 | tf_op jit(solution)/shard_map/pallas_call | solution.py:403
  204.9 1.9 copy.10
